TPU v7x, 32 devices: a whole 2x2x4 slice. The times are simulated.
32 devices in a mesh: tt: 4 (over y, x), sv: 8 (over z, core).
Axes of the slice: x: 2, y: 2, z: 4, core: 2. Of those that a mesh axis runs over, the one named last changes fastest.
Arguments:
- teacher_hidden: bfloat16 [64, 16384], P(None, 'sv'), may hold values from -620 to 620
- teacher_head: bfloat16 [16384, 65536], P('sv', 'tt'), may hold values from -0.046875 to 0.046875
- student_hidden: bfloat16 [64, 4096], P(('tt', 'sv')), may hold values from -42 to 42
- student_head: bfloat16 [4096, 65536], P(None, ('tt', 'sv')), may hold values from -1.5 to 1.5
- targets: int32 [64], replicated, may hold values from 0 to 65535
Outputs:
- loss: float32 [], replicated
- head_grad: bfloat16 [4096, 65536], P(None, ('tt', 'sv'))
- hidden_grad: float32 [64, 4096], P(('tt', 'sv'))
All inputs are finite; a program needn't handle non-finite values.
Results may differ from a plain program's by a relative error of at most 0.0038.
Values may be sent and summed in bfloat16 or wider, within the bound.
A program may use at most 192 MiB of HBM per device.

v0:
```python
import jax
import jax.numpy as jnp
from jax import lax
from jax.sharding import PartitionSpec as P

ce_weight = 0.5


def merged(value, axis, join):
    pieces = jax.tree.map(lambda part: lax.all_gather(part, axis), value)
    head = jax.tree.map(lambda part: part[0], pieces)
    tail = jax.tree.map(lambda part: part[1:], pieces)
    total, _ = lax.scan(lambda total, piece: (join(total, piece), None), head, tail)
    return total


def combine_pair(first, second):
    top = jnp.maximum(first[0], second[0])
    total = first[1] * jnp.exp(first[0] - top) + second[1] * jnp.exp(second[0] - top)
    return (top, total)


def combine_stats(first, second):
    top, total = combine_pair(first[:2], second[:2])
    return (
        top,
        total,
        first[2] + second[2],
        first[3] + second[3],
        first[4] + second[4],
        first[5] + second[5],
    )


def body(teacher_hidden, teacher_head, student_hidden, student_head, targets):
    tokens = teacher_hidden.shape[0]
    vocab_dev = student_head.shape[1]
    rows = teacher_hidden
    logits_t = lax.psum_scatter(
        jnp.dot(rows, teacher_head, preferred_element_type=jnp.float32),
        "sv",
        scatter_dimension=0,
        tiled=True,
    )
    top_t = jnp.max(logits_t, axis=1)
    total_t = jnp.sum(jnp.exp(logits_t - top_t[:, None]), axis=1)
    top_t, total_t = merged((top_t, total_t), "tt", combine_pair)
    log_t = logits_t - (top_t + jnp.log(total_t))[:, None]
    rounded = lax.optimization_barrier(jnp.exp(log_t).astype(jnp.bfloat16))
    entropy = jnp.sum(rounded.astype(jnp.float32) * log_t)
    probs = lax.all_to_all(rounded, "sv", split_axis=1, concat_axis=0, tiled=True)
    hidden_all = lax.all_gather(student_hidden, ("tt", "sv"), axis=0, tiled=True)
    logits_s = jnp.dot(hidden_all, student_head, preferred_element_type=jnp.float32)
    offset = lax.axis_index(("tt", "sv")) * vocab_dev
    columns = offset + lax.broadcasted_iota(jnp.int32, (1, vocab_dev), 1)
    hit = (columns == targets[:, None]).astype(jnp.float32)
    probs_f = probs.astype(jnp.float32)
    top_s = jnp.max(logits_s, axis=1)
    total_s = jnp.sum(jnp.exp(logits_s - top_s[:, None]), axis=1)
    cross = jnp.sum(probs_f * logits_s, axis=1)
    mass = jnp.sum(probs_f, axis=1)
    picked = jnp.sum(hit * logits_s, axis=1)
    top_s, total_s, cross, mass, picked, entropy = merged(
        (top_s, total_s, cross, mass, picked, entropy), ("tt", "sv"), combine_stats
    )
    norm_s = top_s + jnp.log(total_s)
    loss = (
        entropy - jnp.sum(cross - mass * norm_s) + ce_weight * jnp.sum(norm_s - picked)
    ) / tokens
    probs_s = jnp.exp(logits_s - norm_s[:, None])
    grad_logits = ((mass + ce_weight)[:, None] * probs_s - probs_f - ce_weight * hit).astype(
        jnp.bfloat16
    )
    head_grad = lax.dot_general(
        hidden_all, grad_logits, (((0,), (0,)), ((), ())), preferred_element_type=jnp.float32
    ).astype(jnp.bfloat16)
    rows = grad_logits
    hidden_grad = lax.psum_scatter(
        lax.dot_general(
            rows, student_head, (((1,), (1,)), ((), ())), preferred_element_type=jnp.float32
        ),
        ("tt", "sv"),
        scatter_dimension=0,
        tiled=True,
    )
    return (loss, head_grad, hidden_grad)


def solution(mesh):
    placed = (P(None, "sv"), P("sv", "tt"), P(("tt", "sv"), None), P(None, ("tt", "sv")), P())
    return jax.shard_map(
        body,
        mesh=mesh,
        in_specs=placed,
        out_specs=(P(), P(None, ("tt", "sv")), P(("tt", "sv"), None)),
        check_vma=False,
    )
```

profile of v0, /device:TPU:0, one launch (start us, length us, event | category | flops | bytes accessed | tf_op | source)
XLA Modules:
  0.0 430.4 jit_solution(9055010911182725490)
XLA Ops:
  7.2 0.9 copy-done
  8.1 25.4 %fusion.28 = f32[64,16384]{1,0:T(8,128)} fusion(bf16[64,2048]{1,0:T(8,128)(2,1)S(1)} %copy-done, bf16[2048,16384]{1,0:T(8,128)(2,1)} %param.10), kind=kOutput, calls=%fused_computation.49 | convolution fusion | flops 4294967296 | bytes 71565312 | tf_op jit(solution)/shard_map/dot_general | solution.py:40
  33.6 50.7 %all-gather.6 = bf16[32,2,4096]{2,1,0:T(2,128)(2,1)S(1)} all-gather(bf16[1,2,4096]{2,1,0:T(2,128)(2,1)S(1)} %bitcast.87), channel_id=1, replica_groups=mesh['tt'=4,'sv'=8] {'tt','sv'}, dimensions={0}, use_global_device_ids=true | all-gather | bytes 540672 | tf_op jit(solution)/shard_map/all_gather | solution.py:52
  84.5 0.7 dynamic-slice
  85.9 4.8 %reduce-scatter.2.cloned.1.call-done = f32[8,16384]{1,0:T(8,128)} async-done(((f32[64,16384]{1,0:T(8,128)}), f32[8,16384]{1,0:T(8,128)}) %reduce-scatter.2.cloned.1.call-update) | async-done | bytes 524304 | tf_op jit(solution)/shard_map/reduce_scatter | solution.py:39
  90.6 1.4 reduce_max.19
  92.2 1.4 exponential_reduce_fusion
  93.8 10.4 %all-reduce.9 = (f32[32]{0:T(128)S(1)}, f32[32]{0:T(128)S(1)}) all-reduce(f32[32]{0:T(128)S(1)} %dynamic-update-slice.2, f32[32]{0:T(128)S(1)} %dynamic-update-slice.3), channel_id=4, replica_groups=mesh['tt'=4,'sv'=8] {'tt'}, use_global_device_ids=true, to_apply=%add.2 | all-reduce | flops 64 | bytes 512
  104.6 1.9 exponential_convert_fusion
  106.5 3.4 all-to-all-start
  110.0 8.9 %fusion.27 = (f32[64]{0:T(128)S(1)}, f32[64,2048]{1,0:T(8,128)S(1)}) fusion(bf16[64,4096]{1,0:T(8,128)(2,1)S(1)} %reshape.66, bf16[4096,2048]{1,0:T(8,128)(2,1)} %param.12), kind=kOutput, calls=%fused_computation.48 | convolution fusion | flops 1073872896 | bytes 17826048 | tf_op jit(solution)/shard_map/dot_general | solution.py:53
  119.2 1.8 multiply_reduce_fusion
  121.0 0.8 dynamic-update-slice.6
  122.9 40.4 %all-reduce.8 = (f32[2048]{0:T(1024)S(1)}, f32[2048]{0:T(1024)S(1)}, f32[2048]{0:T(1024)S(1)}, f32[2048]{0:T(1024)S(1)}, f32[32]{0:T(128)}) all-reduce(f32[2048]{0:T(1024)S(1)} %dynamic-update-slice, f32[2048]{0:T(1024)S(1)} %dynamic-update-slice.1, f32[2048]{0:T(1024)S(1)} %dynamic-update-slice.4, ...), channel_id=2, replica_groups=mesh['tt'=4,'sv'=8] {'tt','sv'}, use_global_device_ids=true, to_apply=%add | all-reduce | flops 8224 | bytes 65792
  163.8 40.1 %all-gather.7 = f32[32,1,64]{2,1,0:T(1,128)S(1)} all-gather(f32[1,1,64]{2,1,0:T(1,128)S(1)} %reshape.67), channel_id=1, replica_groups=mesh['tt'=4,'sv'=8] {'tt','sv'}, dimensions={0}, use_global_device_ids=true | all-gather | bytes 8448 | tf_op jit(solution)/shard_map/all_gather | solution.py:10
  203.9 0.7 slice.63
  204.9 75.9 %while.33 = (s32[]{:T(128)}, f32[64]{0:T(128)S(1)}, f32[64]{0:T(128)S(1)}, f32[64]{0:T(128)S(1)}, f32[64]{0:T(128)S(1)}, /*index=5*/f32[64]{0:T(128)S(1)}, f32[]...) while((s32[]{:T(128)}, f32[64]{0:T(128)S(1)}, ...), condition=%wide.region_12.13_spmd, body=%wide.region_11.12_spmd.sunk | while | flops 579 | bytes 4013 | solution.py:13
  204.9 0.6 dynamic_slice.79
  280.8 0.6 subtract_reduce_fusion
  281.4 12.1 %fusion.22 = f32[64,4096]{1,0:T(8,128)} fusion(bf16[4096,2048]{1,0:T(8,128)(2,1)} %param.12, bf16[8,8,2048]{2,0,1:T(8,128)(2,1)S(1)} %all-to-all-done, f32[64,2048]{1,0:T(8,128)S(1)} %get-tuple-element.175, f32[64]{0:T(128)S(1)} %get-tuple-element.169, f32[64]{0:T(128)S(1)} %get-tuple-element.173, s32[2048]{0:T(1024)S(1)} %iota_add_fusion, s32[64]{0:T(128)S(1)} %copy-done.3), kind=kOutput, calls=%fused_computation.47 | convolution fusion | flops 1074790400 | bytes 18621184 | tf_op jit(solution)/shard_map/dot_general | solution.py:79
  293.5 8.3 %convert_bitcast_fusion = bf16[4096,2048]{0,1:T(8,128)(2,1)} fusion(bf16[64,4096]{1,0:T(8,128)(2,1)S(1)} %reshape.66, bf16[8,8,2048]{2,0,1:T(8,128)(2,1)S(1)} %all-to-all-done, f32[64,2048]{1,0:T(8,128)S(1)} %get-tuple-element.175, f32[64]{0:T(128)S(1)} %get-tuple-element.169, f32[64]{0:T(128)S(1)} %get-tuple-element.173, s32[2048]{0:T(1024)S(1)} %iota_add_fusion, ...), kind=kOutput, calls=%fused_computation.23 | convolution fusion | flops 1083179008 | bytes 18096896 | tf_op jit(solution)/shard_map/dot_general | solution.py:74
  301.8 22.5 %copy.9 = bf16[4096,2048]{1,0:T(8,128)(2,1)} copy(bf16[4096,2048]{0,1:T(8,128)(2,1)} %convert_bitcast_fusion) | data formatting | bytes 33554432
  326.2 94.7 %all-reduce.12.cloned.1.call-done = f32[64,4096]{1,0:T(8,128)} async-done(((f32[64,4096]{1,0:T(8,128)}), f32[64,4096]{1,0:T(8,128)}) %all-reduce.12.cloned.1.call-update) | async-done | bytes 1048592
  420.9 1.5 constant_dynamic-slice_fusion.7
  (148 shorter events, 22.6 us)
Async XLA Ops:
  7.2 1.0 copy-start
  7.2 77.3 %copy-start.4 = (u32[32]{0:T(128)S(1)}, u32[32]{0:T(128)}, u32[]{:S(2)}) copy-start(u32[32]{0:T(128)} %constant.57) | copy-start | bytes 388
  7.2 26.4 %copy-start.2 = (bf16[2,4096]{1,0:T(2,128)(2,1)S(1)}, bf16[2,4096]{1,0:T(2,128)(2,1)}, u32[]{:S(2)}) copy-start(bf16[2,4096]{1,0:T(2,128)(2,1)} %param.11) | copy-start | bytes 49156
  7.2 83.4 %reduce-scatter.2.cloned.1.call-start = ((), (), s32[]{:S(2)}) async-start(), calls=%async_computation.2 | async-start | bytes 4718592 | tf_op jit(solution)/shard_map/reduce_scatter | solution.py:39
  33.5 88.2 %copy-start.3 = (s32[64]{0:T(128)S(1)}, s32[64]{0:T(128)}, u32[]{:S(2)}) copy-start(s32[64]{0:T(128)} %param.13) | copy-start | bytes 772
  90.6 28.6 %copy-start.1 = (f32[8,16384]{1,0:T(8,128)S(1)}, f32[8,16384]{1,0:T(8,128)}, u32[]{:S(2)}) copy-start(f32[8,16384]{1,0:T(8,128)} %reduce-scatter.2.cloned.1.call-done) | copy-start | bytes 1572868
  106.5 15.2 %all-to-all-start = ((bf16[8,8,2048]{2,0,1:T(8,128)(2,1)}), bf16[8,8,2048]{2,0,1:T(8,128)(2,1)S(1)}, u32[]{:S(2)}, u32[]{:S(2)}) async-start(bf16[8,8,2048]{2,0,1:T(8,128)(2,1)} %bitcast.10), calls=%async_computation.1 | async-start | bytes 524288 | tf_op jit(solution)/shard_map/all_to_all | solution.py:51
  110.0 310.9 %all-reduce.12.cloned.1.call-start = ((), (), s32[]{:S(2)}) async-start(), calls=%async_computation.3 | async-start | bytes 2097152
Sparse Core Ops, SparseCore 0:
  33.7 56.9 reduce-scatter.1
  293.6 127.1 all-reduce.11
where the time goes:
time: 432 us; the launch traced here: 430 us
  blocking collectives  142 us (33%)
  waiting for transfers between devices  99.5 us (23%)
  loops' own time  56.3 us (13%)
  matrix products  54.7 us (13%)
  local copies, waits for them, and re-layouts  47.8 us (11%)
  between operations  17.9 us (4%)
  other arithmetic  9.14 us (2%)
    unnamed x3, waiting for transfers between devices  94.7 us
    another operation x2, loops' own time, merged(): lax.scan(lambda total, piece: (join(total, piece), None), head, tail)  56.3 us
    unnamed x2, blocking collectives  50.7 us
    all_gather x1, blocking collectives, body(): lax.all_gather(student_hidden, ('tt', 'sv'), axis=0, tiled=True)  50.7 us
    all_gather x1, blocking collectives, merged(): pieces = jax.tree.map(lambda part: lax.all_gather(part, axis), value)  40.1 us
    unnamed x30, local copies, waits for them, and re-layouts  28.2 us
    dot_general x1, matrix products, body(): jnp.dot(rows, teacher_head, preferred_element_type=jnp.float32)  25.4 us
    dynamic_slice x31, local copies, waits for them, and re-layouts, merged(): lax.scan(lambda total, piece: (join(total, piece), None), head, tail)  18.1 us
  transfers between devices with their start and end apart: 3, of which 2 were waited for; matrix products, arithmetic and copies ran while one was open for 10% of the time, Pallas kernels for 0%

commit v1 on v0

v1 whole, which is shorter than its diff:
```python
import functools

import jax
import jax.numpy as jnp
from jax import lax
from jax.experimental import pallas as pl
from jax.experimental.pallas import tpu as pltpu
from jax.sharding import PartitionSpec as P

MESH = pl.DeviceIdType.MESH
ce_weight = 0.5
depth = 6


def visit_order(nz):
    table = []
    for z in range(nz):
        right, left = list(range(nz - 1, z, -1)), list(range(z))
        first, second = (right, left) if len(right) >= len(left) else (left, right)
        order = []
        while first or second:
            if first:
                order.append(first.pop(0))
            if second:
                order.append(second.pop(0))
        table.append(order + [z])
    return table


def lookup(table, row, column):
    value = jnp.int32(0)
    for r, entries in enumerate(table):
        for c, entry in enumerate(entries):
            if entry:
                value = jnp.where((row == r) & (column == c), jnp.int32(entry), value)
    return value


def kernel(
    ntt, nv, nq,
    t_hidden, t_head, s_hidden, s_head, targets,
    loss_ref, hid_ref, grad_ref, hgrad_ref,
    t_buf, w_buf, mine, sib_out, sib_in, line_in, logits_t, logits_s,
    hid_all, hid_f, stat_all, hg_out, hg_in, hg_own, tt_out, tt_in, z_out, z_in, c_out, c_in,
    t_sem, w_sem, sib_send, sib_recv, line_send, line_recv,
    hid_send, hid_recv, stat_send, stat_recv, hg_send, hg_recv, tt_send, tt_recv, z_send, z_recv,
):
    nz = nv // 2
    tt, sv = lax.axis_index("tt"), lax.axis_index("sv")
    z, core = sv // 2, sv % 2
    tokens = t_hidden.shape[0]
    vd = s_head.shape[1]
    ds = s_head.shape[0]
    cw = vd // nq
    steps = nz * nq
    table = visit_order(nz)

    def other_z(k):
        return lax.rem(z + k, nz)

    def other_tt(k):
        return lax.rem(tt + k, ntt)

    def push(src, dst, send, recv, where):
        return pltpu.make_async_remote_copy(
            src_ref=src, dst_ref=dst, send_sem=send, recv_sem=recv, device_id=where, device_id_type=MESH
        )

    sibling = {"sv": z * 2 + (1 - core)}

    def piece(i):
        s, half = i // 2, i % 2
        dest = lookup(table, z, s // nq)
        who = jnp.where(half == 0, 1 - core, core)
        start = pl.multiple_of((dest * 2 + who) * vd + (s % nq) * cw, 128)
        slot = lax.rem(i, depth)
        return pltpu.make_async_copy(t_head.at[:, pl.ds(start, cw)], t_buf.at[slot], t_sem.at[slot])

    for i in range(min(depth, 2 * steps)):
        piece(jnp.int32(i)).start()
    student = pltpu.make_async_copy(s_head, w_buf, w_sem)

    barrier = pltpu.get_barrier_semaphore()
    pl.semaphore_signal(barrier, inc=1, device_id=sibling, device_id_type=MESH)
    for k in range(1, nz):
        pl.semaphore_signal(barrier, inc=1, device_id={"sv": other_z(k) * 2 + core}, device_id_type=MESH)
    for k in range(1, ntt):
        pl.semaphore_signal(barrier, inc=1, device_id={"tt": other_tt(k)}, device_id_type=MESH)
    pl.semaphore_wait(barrier, nz + ntt - 1)

    def gather_z(buf, send, recv):
        return [
            push(buf.at[core, tt, z], buf.at[core, tt, z], send.at[k], recv.at[z], {"sv": other_z(k) * 2 + core})
            for k in range(1, nz)
        ]

    def gather_z_wait(buf, send, recv):
        for k in range(1, nz):
            p = other_z(k)
            push(buf.at[core, tt, p], buf.at[core, tt, p], send.at[k], recv.at[p], {"sv": p * 2 + core}).wait_recv()

    def gather_tt(buf, send, recv):
        return [
            push(buf.at[core, tt], buf.at[core, tt], send.at[nz + k], recv.at[nz + tt], {"tt": other_tt(k)})
            for k in range(1, ntt)
        ]

    def gather_tt_wait(buf, send, recv):
        for k in range(1, ntt):
            p = other_tt(k)
            push(buf.at[core, p], buf.at[core, p], send.at[nz + k], recv.at[nz + p], {"tt": p}).wait_recv()

    def gather_core(buf, send, recv):
        return push(buf.at[core], buf.at[core], send.at[0], recv.at[nz + ntt], sibling)

    def gather_core_wait(buf, send, recv):
        push(buf.at[1 - core], buf.at[1 - core], send.at[0], recv.at[nz + ntt], sibling).wait_recv()

    def start_all(copies):
        for copy in copies:
            copy.start()

    def gather_sent(buf, send, recv):
        for copy in gather_z(buf, send, recv) + gather_tt(buf, send, recv) + [gather_core(buf, send, recv)]:
            copy.wait_send()

    hid_gather = (hid_all, hid_send, hid_recv)
    hid_all[core, tt, z] = s_hidden[...].astype(jnp.float32)
    start_all(gather_z(*hid_gather))

    def sib_copy(s):
        dest, q = lookup(table, z, s // nq), s % nq
        return push(sib_out.at[dest, q], sib_in.at[dest, q], sib_send.at[s], sib_recv.at[s], sibling)

    def line_copy(s):
        dest, q = lookup(table, z, s // nq), s % nq
        side = jnp.where(dest > z, 0, 1)
        onto = jnp.where(dest > z, z + 1, z - 1)
        return push(
            mine.at[dest, q], line_in.at[side, dest, q], line_send.at[s], line_recv.at[side, dest, q],
            {"sv": onto * 2 + core},
        )

    def line_arrived(side, dest, q):
        ref = line_in.at[side, dest, q]
        push(ref, ref, line_send.at[0], line_recv.at[side, dest, q], sibling).wait_recv()

    def pair(s):
        sib_copy(s).wait_recv()
        dest, q = lookup(table, z, s // nq), s % nq
        mine[dest, q] += sib_in[dest, q]

    def forward(s):
        dest, q = lookup(table, z, s // nq), s % nq
        side = jnp.where(dest > z, 0, 1)
        upstream = jnp.where(dest > z, z > 0, z < nz - 1)

        @pl.when(upstream)
        def _():
            line_arrived(side, dest, q)
            mine[dest, q] += line_in[side, dest, q]

        line_copy(s).start()

    outer = (nz - 1) * nq
    at_end = (z == 0) | (z == nz - 1)

    @pl.loop(0, steps)
    def _(s):
        dest, q = lookup(table, z, s // nq), s % nq
        for half, target in ((0, sib_out), (1, mine)):
            i = 2 * s + half
            piece(i).wait()
            target[dest, q] = jnp.dot(
                t_hidden[...], t_buf[lax.rem(i, depth)], preferred_element_type=jnp.float32
            )
            if half == 0:
                sib_copy(s).start()

            @pl.when(i + depth < 2 * steps)
            def _():
                piece(i + depth).start()

        @pl.when(s == max(0, steps - 4))
        def _():
            student.start()

        @pl.when(s >= 1)
        def _():
            pair(s - 1)

        late = jnp.where(at_end, s - 1, s - 2)

        @pl.when((late >= 0) & (late < outer))
        def _():
            forward(late)

        @pl.when(s == steps // 4)
        def _():
            gather_z_wait(*hid_gather)
            start_all(gather_tt(*hid_gather))

        @pl.when(s == steps // 2)
        def _():
            gather_tt_wait(*hid_gather)
            gather_core(*hid_gather).start()

    pair(jnp.int32(steps - 1))
    for late in range(max(0, steps - 2), outer):

        @pl.when(jnp.logical_not(at_end) | (late >= steps - 1))
        def _():
            forward(jnp.int32(late))

    gather_core_wait(*hid_gather)
    rows = s_hidden.shape[0]
    for a in range(ntt):
        for b in range(nz):
            for c in range(2):
                at = (a * nv + b * 2 + c) * rows
                hid_f[at : at + rows, :] = hid_all[c, a, b]
    hid_ref[...] = hid_f[...].astype(jnp.bfloat16)

    student.wait()

    @pl.loop(0, nq)
    def _(n):
        logits_s[n] = jnp.dot(
            hid_ref[...], w_buf[:, pl.ds(pl.multiple_of(n * cw, 128), cw)], preferred_element_type=jnp.float32
        )

    for q in range(nq):
        logits_t[q] = mine[z, q]
        for side, there in ((0, z > 0), (1, z < nz - 1)):

            @pl.when(there)
            def _():
                line_arrived(side, z, q)
                logits_t[q] += line_in[side, z, q]

    offset = (tt * nv + sv) * vd
    lanes = stat_all.shape[-1]

    def hits(q):
        columns = offset + q * cw + lax.broadcasted_iota(jnp.int32, (tokens, cw), 1)
        return (columns == targets[...]).astype(jnp.float32)

    def over(function, join):
        return functools.reduce(join, [function(q) for q in range(nq)])

    def add(a, b):
        return a + b

    def total(values):
        return jnp.sum(values, axis=1, keepdims=True)

    top_t = over(lambda q: jnp.max(logits_t[q], axis=1, keepdims=True), jnp.maximum)
    top_s = over(lambda q: jnp.max(logits_s[q], axis=1, keepdims=True), jnp.maximum)
    sums = [jnp.zeros((tokens, 1), jnp.float32) for _ in range(5)]
    for q in range(nq):
        lt, ls = logits_t[q] - top_t, logits_s[q]
        et = jnp.exp(lt)
        here = (et, et * ls, et * lt, jnp.exp(ls - top_s), hits(q) * ls)
        sums = [old + total(new) for old, new in zip(sums, here)]
    eye = lax.broadcasted_iota(jnp.int32, (tokens, lanes), 0) == lax.broadcasted_iota(jnp.int32, (tokens, lanes), 1)

    def to_row(column):
        return jnp.sum(jnp.where(eye, column, 0.0), axis=0, keepdims=True)

    def to_column(row):
        return jnp.sum(jnp.where(eye, row, 0.0), axis=1, keepdims=True)

    stats = [top_t, sums[0], sums[1], sums[2], top_s, sums[3], sums[4]]
    stat_all[core, tt, z] = jnp.concatenate(
        [to_row(x) for x in stats] + [jnp.zeros((1, lanes), jnp.float32)], axis=0
    )
    stat_gather = (stat_all, stat_send, stat_recv)
    start_all(gather_z(*stat_gather))
    gather_z_wait(*stat_gather)
    start_all(gather_tt(*stat_gather))
    gather_tt_wait(*stat_gather)
    gather_core(*stat_gather).start()
    gather_core_wait(*stat_gather)

    every = stat_all[...].reshape((2 * ntt * nz, 8, lanes))
    peak = jnp.max(every, axis=0)
    scale = jnp.exp(every - peak[None])
    wt, ws = scale[:, 0, :], scale[:, 4, :]
    real = lax.broadcasted_iota(jnp.int32, (1, lanes), 1) < tokens

    def joined(values):
        return jnp.where(real, jnp.sum(values, axis=0, keepdims=True), 1.0)

    sum_t = joined(wt * every[:, 1, :])
    sum_s = joined(ws * every[:, 5, :])
    log_t = jnp.log(sum_t)
    mass = joined(wt * every[:, 1, :]) / sum_t
    cross = joined(wt * every[:, 2, :]) / sum_t
    shifted = every[:, 3, :] + (every[:, 0, :] - peak[0:1]) * every[:, 1, :]
    entropy = joined(wt * shifted) / sum_t - mass * log_t
    norm_s = peak[4:5] + jnp.log(sum_s)
    picked = joined(every[:, 6, :])
    per_row = entropy - (cross - mass * norm_s) + ce_weight * (norm_s - picked)
    loss_ref[0, 0] = jnp.sum(jnp.where(real, per_row, 0.0)) / tokens

    norm_t_col = to_column(peak[0:1] + log_t)
    norm_s_col = to_column(norm_s)
    mass_col = to_column(mass)
    for q in range(nq):
        probs = jnp.exp(logits_t[q] - norm_t_col).astype(jnp.bfloat16).astype(jnp.float32)
        grad = (mass_col + ce_weight) * jnp.exp(logits_s[q] - norm_s_col) - probs - ce_weight * hits(q)
        grad_ref[:, q * cw : (q + 1) * cw] = grad.astype(jnp.bfloat16)

    half = ds // 2
    width = 512
    for who, target in ((1 - core, hg_out), (core, hg_own)):

        @pl.loop(0, half // width)
        def _(n):
            start = pl.multiple_of(who * half + n * width, 128)
            target[:, pl.ds(pl.multiple_of(n * width, 128), width)] = lax.dot_general(
                grad_ref[...], w_buf[pl.ds(start, width), :], (((1,), (1,)), ((), ())),
                preferred_element_type=jnp.float32,
            )

        if target is hg_out:
            push(hg_out, hg_in, hg_send.at[0], hg_recv.at[0], sibling).start()
    hg_pair = push(hg_out, hg_in, hg_send.at[0], hg_recv.at[0], sibling)
    hg_pair.wait_recv()
    group = tokens // ntt
    for a in range(ntt):
        part = slice(a * group, (a + 1) * group)
        tt_out[a] = hg_own[part, :] + hg_in[part, :]
    copies = [
        push(tt_out.at[other_tt(k)], tt_in.at[tt], tt_send.at[k], tt_recv.at[tt], {"tt": other_tt(k)})
        for k in range(1, ntt)
    ]
    start_all(copies)
    here = tt_out[tt]
    for k in range(1, ntt):
        p = other_tt(k)
        push(tt_in.at[p], tt_in.at[p], tt_send.at[k], tt_recv.at[p], {"tt": p}).wait_recv()
        here = here + tt_in[p]
    for b in range(nz):
        z_out[b] = here[b * 2 * rows : (b + 1) * 2 * rows, :]
    z_copies = [
        push(z_out.at[other_z(k)], z_in.at[z], z_send.at[k], z_recv.at[z], {"sv": other_z(k) * 2 + core})
        for k in range(1, nz)
    ]
    start_all(z_copies)
    here = z_out[z]
    for k in range(1, nz):
        p = other_z(k)
        push(z_in.at[p], z_in.at[p], z_send.at[k], z_recv.at[p], {"sv": p * 2 + core}).wait_recv()
        here = here + z_in[p]
    for c in range(2):
        c_out[c] = here[c * rows : (c + 1) * rows, :]
    last = push(c_out.at[1 - core], c_in, hg_send.at[1], hg_recv.at[1], sibling)
    last.start()
    hgrad_ref[:, pl.ds(pl.multiple_of(core * half, 128), half)] = c_out[core]
    last.wait_recv()
    hgrad_ref[:, pl.ds(pl.multiple_of((1 - core) * half, 128), half)] = c_in[...]

    last.wait_send()
    hg_pair.wait_send()
    for copy in copies + z_copies:
        copy.wait_send()
    gather_sent(*hid_gather)
    gather_sent(*stat_gather)

    @pl.loop(0, steps)
    def _(s):
        sib_copy(s).wait_send()

        @pl.when(s < outer)
        def _():
            line_copy(s).wait_send()


def head_kernel(hid_ref, grad_ref, out_ref):
    out_ref[...] = lax.dot_general(
        hid_ref[...], grad_ref[...], (((0,), (0,)), ((), ())), preferred_element_type=jnp.float32
    ).astype(out_ref.dtype)


def body(ntt, nv, teacher_hidden, teacher_head, student_hidden, student_head, targets):
    f32, bf16 = jnp.float32, jnp.bfloat16
    tokens, dt = teacher_hidden.shape
    rows = student_hidden.shape[0]
    ds, vd = student_head.shape
    nz = nv // 2
    cw = min(vd, 512)
    nq = vd // cw
    steps = nz * nq
    lanes = -(-tokens // 128) * 128
    half = ds // 2
    sems = pltpu.SemaphoreType.DMA
    vmem = pl.BlockSpec(memory_space=pltpu.VMEM)
    hbm = pl.BlockSpec(memory_space=pl.ANY)
    shards = (nz, nq, tokens, cw)
    peers = nz + ntt + 1
    loss, hid, grad, hidden_grad = pl.pallas_call(
        functools.partial(kernel, ntt, nv, nq),
        out_shape=(
            jax.ShapeDtypeStruct((1, 1), f32),
            jax.ShapeDtypeStruct((tokens, ds), bf16),
            jax.ShapeDtypeStruct((tokens, vd), bf16),
            jax.ShapeDtypeStruct((rows, ds), f32),
        ),
        in_specs=[vmem, hbm, vmem, hbm, vmem],
        out_specs=(pl.BlockSpec(memory_space=pltpu.SMEM), vmem, vmem, vmem),
        scratch_shapes=[
            pltpu.VMEM((depth, dt, cw), bf16),
            pltpu.VMEM((ds, vd), bf16),
            pltpu.VMEM(shards, f32),
            pltpu.VMEM(shards, f32),
            pltpu.VMEM(shards, f32),
            pltpu.VMEM((2,) + shards, f32),
            pltpu.VMEM(shards[1:], f32),
            pltpu.VMEM(shards[1:], f32),
            pltpu.VMEM((2, ntt, nz, rows, ds), f32),
            pltpu.VMEM((tokens, ds), f32),
            pltpu.VMEM((2, ntt, nz, 8, lanes), f32),
            pltpu.VMEM((tokens, half), f32),
            pltpu.VMEM((tokens, half), f32),
            pltpu.VMEM((tokens, half), f32),
            pltpu.VMEM((ntt, tokens // ntt, half), f32),
            pltpu.VMEM((ntt, tokens // ntt, half), f32),
            pltpu.VMEM((nz, 2 * rows, half), f32),
            pltpu.VMEM((nz, 2 * rows, half), f32),
            pltpu.VMEM((2, rows, half), f32),
            pltpu.VMEM((rows, half), f32),
            sems((depth,)),
            sems,
            sems((steps,)),
            sems((steps,)),
            sems((steps,)),
            sems((2, nz, nq)),
            sems((peers,)),
            sems((peers,)),
            sems((peers,)),
            sems((peers,)),
            sems((2,)),
            sems((2,)),
            sems((ntt,)),
            sems((ntt,)),
            sems((nz,)),
            sems((nz,)),
        ],
        compiler_params=pltpu.CompilerParams(
            collective_id=0, has_side_effects=True, vmem_limit_bytes=60 * 2**20
        ),
    )(teacher_hidden, teacher_head, student_hidden, student_head, targets.reshape(tokens, 1))
    block = 512
    head_grad = pl.pallas_call(
        head_kernel,
        grid=(ds // block,),
        out_shape=jax.ShapeDtypeStruct((ds, vd), bf16),
        in_specs=[
            pl.BlockSpec((tokens, block), lambda i: (0, i)),
            pl.BlockSpec((tokens, vd), lambda i: (0, 0)),
        ],
        out_specs=pl.BlockSpec((block, vd), lambda i: (i, 0)),
        compiler_params=pltpu.CompilerParams(vmem_limit_bytes=32 * 2**20),
    )(hid, grad)
    return (loss.reshape(()), head_grad, hidden_grad)


def solution(mesh):
    placed = (P(None, "sv"), P("sv", "tt"), P(("tt", "sv"), None), P(None, ("tt", "sv")), P())
    return jax.shard_map(
        functools.partial(body, mesh.shape["tt"], mesh.shape["sv"]),
        mesh=mesh,
        in_specs=placed,
        out_specs=(P(), P(None, ("tt", "sv")), P(("tt", "sv"), None)),
        check_vma=False,
    )
```

time: 432 us -> 88.5 us (0.20)
  blocking collectives: 142 us -> 0 us
  waiting for transfers between devices: 99.5 us -> 0 us
  Pallas kernels: 0 us -> 82 us
  loops' own time: 56.3 us -> 0 us
  matrix products: 54.7 us -> 0 us
  local copies, waits for them, and re-layouts: 47.8 us -> 3.96 us
  between operations: 17.9 us -> 2.35 us
  other arithmetic: 9.14 us -> 0 us
    unnamed x3 -> x0, waiting for transfers between devices: 94.7 us -> none
    all_gather x2 -> x0, blocking collectives: 90.8 us -> none  [the longest x1 50.7 us: body(): lax.all_gather(student_hidden, ('tt', 'sv'), axis=0, tiled=True)]
    pallas_call x0 -> x2, Pallas kernels: none -> 82 us  [the longest x1 73 us: body(): pl.pallas_call(functools.partial(kernel, ntt, nv, nq), out_shape=(jax.Sha...]
    another operation x2 -> x0, loops' own time: 56.3 us -> none  [merged(): lax.scan(lambda total, piece: (join(total, piece), None), head, tail)]
    dot_general x4 -> x0, matrix products: 54.7 us -> none  [the longest x1 25.4 us: body(): jnp.dot(rows, teacher_head, preferred_element_type=jnp.float32)]
    unnamed x2 -> x0, blocking collectives: 50.7 us -> none
    unnamed x30 -> x7, local copies, waits for them, and re-layouts: 28.2 us -> 2.61 us
    dynamic_slice x31 -> x0, local copies, waits for them, and re-layouts: 18.1 us -> none  [merged(): lax.scan(lambda total, piece: (join(total, piece), None), head, tail)]
  transfers between devices with their start and end apart: 3 -> 0, of which waited for: 2 -> 0; matrix products, arithmetic and copies ran while one was open for 10% -> 0% of each run, Pallas kernels for 0% -> 0%
where the time goes in v1:
time: 88.5 us; the launch traced here: 88.3 us
  Pallas kernels  82 us (93%)
  local copies, waits for them, and re-layouts  3.96 us (4%)
  between operations  2.35 us (3%)
    pallas_call x1, Pallas kernels, body(): pl.pallas_call(functools.partial(kernel, ntt, nv, nq), out_shape=(jax.Sha...  73 us
    pallas_call x1, Pallas kernels, body(): pl.pallas_call(head_kernel, grid=(ds // block,), out_shape=jax.ShapeDtype...  8.98 us
    unnamed x7, local copies, waits for them, and re-layouts  2.61 us

profile of v1, /device:TPU:0, one launch (start us, length us, event | category | flops | bytes accessed | tf_op | source)
XLA Modules:
  0.0 88.3 jit_solution(1890103906436429339)
XLA Ops:
  0.6 1.4 %copy.8.targets = s32[64,1]{1,0:T(8,128)} copy(s32[64,1]{0,1:T(1,128)} %bitcast.2) | data formatting | bytes 512 | tf_op jit(solution)/shard_map/reshape | solution.py:453
  2.0 73.0 %shard_map.76 = (f32[1,1]{1,0:T(1,128)}, bf16[64,4096]{1,0:T(8,128)(2,1)}, bf16[64,2048]{1,0:T(8,128)(2,1)}, f32[2,4096]{1,0:T(2,128)}) custom-call(bf16[64,2048]{1,0:T(8,128)(2,1)} %t_hidden.1, bf16[2048,16384]{1,0:T(8,128)(2,1)} %t_head.1, bf16[2,4096]{1,0:T(2,128)(2,1)} %s_hidden.1, bf16[4096,2048]{1,0:T(8,128)(2,1)} %s_head.1, s32[64,1]{1,0:T(8,128)} %copy.8.targets), custom_call_target="tpu_custom_call" | custom-call | tf_op jit(solution)/shard_map/pallas_call | solution.py:402
  75.0 0.0 copy-start
  75.0 1.0 %copy-done = bf16[64,4096]{1,0:T(8,128)(2,1)S(1)} copy-done((bf16[64,4096]{1,0:T(8,128)(2,1)S(1)}, bf16[64,4096]{1,0:T(8,128)(2,1)}, u32[]{:S(2)}) %copy-start) | copy-done | bytes 524312
  76.0 0.0 copy-start.1
  76.0 0.9 %copy-done.1 = bf16[64,2048]{1,0:T(8,128)(2,1)S(1)} copy-done((bf16[64,2048]{1,0:T(8,128)(2,1)S(1)}, bf16[64,2048]{1,0:T(8,128)(2,1)}, u32[]{:S(2)}) %copy-start.1) | copy-done | bytes 262168
  77.0 0.0 copy-start.2
  77.0 9.0 %shard_map.77 = bf16[4096,2048]{1,0:T(8,128)(2,1)} custom-call(bf16[64,4096]{1,0:T(8,128)(2,1)S(1)} %copy-done, bf16[64,2048]{1,0:T(8,128)(2,1)S(1)} %copy-done.1), custom_call_target="tpu_custom_call" | custom-call | tf_op jit(solution)/shard_map/pallas_call | solution.py:455
  86.5 0.0 copy-done.2
  86.5 0.6 copy.12
Async XLA Ops:
  75.0 1.0 %copy-start = (bf16[64,4096]{1,0:T(8,128)(2,1)S(1)}, bf16[64,4096]{1,0:T(8,128)(2,1)}, u32[]{:S(2)}) copy-start(bf16[64,4096]{1,0:T(8,128)(2,1)} %get-tuple-element.8.hid_ref) | copy-start | bytes 1572868
  76.0 0.9 %copy-start.1 = (bf16[64,2048]{1,0:T(8,128)(2,1)S(1)}, bf16[64,2048]{1,0:T(8,128)(2,1)}, u32[]{:S(2)}) copy-start(bf16[64,2048]{1,0:T(8,128)(2,1)} %get-tuple-element.9.grad_ref) | copy-start | bytes 786436
  77.0 9.5 %copy-start.2 = (f32[2,4096]{1,0:T(2,128)S(1)}, f32[2,4096]{1,0:T(2,128)}, u32[]{:S(2)}) copy-start(f32[2,4096]{1,0:T(2,128)} %get-tuple-element.16) | copy-start | bytes 98308

commit v2 on v1

v2 whole, which is shorter than its diff:
```python
import functools

import jax
import jax.numpy as jnp
from jax import lax
from jax.experimental import pallas as pl
from jax.experimental.pallas import tpu as pltpu
from jax.sharding import PartitionSpec as P

MESH = pl.DeviceIdType.MESH
ce_weight = 0.5
depth = 6
lag = 5


def visit_order(nz):
    table = []
    for z in range(nz):
        right, left = list(range(nz - 1, z, -1)), list(range(z))
        first, second = (right, left) if len(right) >= len(left) else (left, right)
        order = []
        while first or second:
            if first:
                order.append(first.pop(0))
            if second:
                order.append(second.pop(0))
        table.append(order + [z])
    return table


def lookup(table, row, column):
    value = jnp.int32(0)
    for r, entries in enumerate(table):
        for c, entry in enumerate(entries):
            if entry:
                value = jnp.where((row == r) & (column == c), jnp.int32(entry), value)
    return value


def kernel(
    ntt, nv, nq,
    t_hidden, t_head, s_hidden, s_head, targets,
    loss_ref, hid_t_ref, grad_ref, hgrad_ref,
    t_buf, w_buf, mine, sib_out, sib_in, line_in, logits_t, logits_s,
    hid_all, hid_f, hid_ref, stat_all, hg_out, hg_in, hg_own, tt_out, tt_in, z_out, z_in, c_out, c_in,
    t_sem, w_sem, sib_send, sib_recv, line_send, line_recv,
    hid_send, hid_recv, stat_send, stat_recv, hg_send, hg_recv, tt_send, tt_recv, z_send, z_recv,
):
    nz = nv // 2
    tt, sv = lax.axis_index("tt"), lax.axis_index("sv")
    z, core = sv // 2, sv % 2
    tokens = t_hidden.shape[0]
    vd = s_head.shape[1]
    ds = s_head.shape[0]
    cw = vd // nq
    steps = nz * nq
    table = visit_order(nz)

    def other_z(k):
        return lax.rem(z + k, nz)

    def other_tt(k):
        return lax.rem(tt + k, ntt)

    here_at = core * ntt + tt

    def beside(k):
        at = lax.rem(here_at + k, 2 * ntt)
        return at, {"tt": lax.rem(at, ntt), "sv": z * 2 + at // ntt}

    def push(src, dst, send, recv, where):
        return pltpu.make_async_remote_copy(
            src_ref=src, dst_ref=dst, send_sem=send, recv_sem=recv, device_id=where, device_id_type=MESH
        )

    sibling = {"sv": z * 2 + (1 - core)}

    def piece(i):
        s, half = i // 2, i % 2
        dest = lookup(table, z, s // nq)
        who = jnp.where(half == 0, 1 - core, core)
        start = pl.multiple_of((dest * 2 + who) * vd + (s % nq) * cw, 128)
        slot = lax.rem(i, depth)
        return pltpu.make_async_copy(t_head.at[:, pl.ds(start, cw)], t_buf.at[slot], t_sem.at[slot])

    for i in range(min(depth, 2 * steps)):
        piece(jnp.int32(i)).start()
    student = pltpu.make_async_copy(s_head, w_buf, w_sem)

    barrier = pltpu.get_barrier_semaphore()
    for k in range(1, nz):
        pl.semaphore_signal(barrier, inc=1, device_id={"sv": other_z(k) * 2 + core}, device_id_type=MESH)
    for k in range(1, 2 * ntt):
        pl.semaphore_signal(barrier, inc=1, device_id=beside(k)[1], device_id_type=MESH)
    pl.semaphore_wait(barrier, nz + 2 * ntt - 2)

    def gather_z(buf, send, recv):
        return [
            push(
                buf.at[here_at, z], buf.at[here_at, z], send.at[k], recv.at[z], {"sv": other_z(k) * 2 + core}
            )
            for k in range(1, nz)
        ]

    def gather_z_wait(buf, send, recv):
        for k in range(1, nz):
            p = other_z(k)
            ref = buf.at[here_at, p]
            push(ref, ref, send.at[k], recv.at[p], {"sv": p * 2 + core}).wait_recv()

    def gather_rest(buf, send, recv):
        return [
            push(buf.at[here_at], buf.at[here_at], send.at[nz + k], recv.at[nz + here_at], beside(k)[1])
            for k in range(1, 2 * ntt)
        ]

    def gather_rest_wait(buf, send, recv):
        for k in range(1, 2 * ntt):
            at, where = beside(k)
            push(buf.at[at], buf.at[at], send.at[nz + k], recv.at[nz + at], where).wait_recv()

    def start_all(copies):
        for copy in copies:
            copy.start()

    def gather_sent(buf, send, recv):
        for copy in gather_z(buf, send, recv) + gather_rest(buf, send, recv):
            copy.wait_send()

    hid_gather = (hid_all, hid_send, hid_recv)
    hid_all[here_at, z] = s_hidden[...].astype(jnp.float32)
    start_all(gather_z(*hid_gather))

    def sib_copy(s):
        dest, q = lookup(table, z, s // nq), s % nq
        return push(sib_out.at[dest, q], sib_in.at[dest, q], sib_send.at[s], sib_recv.at[s], sibling)

    def line_copy(s):
        dest, q = lookup(table, z, s // nq), s % nq
        side = jnp.where(dest > z, 0, 1)
        onto = jnp.where(dest > z, z + 1, z - 1)
        return push(
            mine.at[dest, q], line_in.at[side, dest, q], line_send.at[s], line_recv.at[side, dest, q],
            {"sv": onto * 2 + core},
        )

    def line_arrived(side, dest, q):
        ref = line_in.at[side, dest, q]
        push(ref, ref, line_send.at[0], line_recv.at[side, dest, q], sibling).wait_recv()

    def pair(s):
        sib_copy(s).wait_recv()
        dest, q = lookup(table, z, s // nq), s % nq
        mine[dest, q] += sib_in[dest, q]

    def forward(s):
        dest, q = lookup(table, z, s // nq), s % nq
        side = jnp.where(dest > z, 0, 1)
        upstream = jnp.where(dest > z, z > 0, z < nz - 1)

        @pl.when(upstream)
        def _():
            line_arrived(side, dest, q)
            mine[dest, q] += line_in[side, dest, q]

        line_copy(s).start()

    outer = (nz - 1) * nq
    at_end = (z == 0) | (z == nz - 1)

    @pl.loop(0, steps)
    def _(s):
        dest, q = lookup(table, z, s // nq), s % nq
        for half, target in ((0, sib_out), (1, mine)):
            i = 2 * s + half
            piece(i).wait()
            target[dest, q] = jnp.dot(
                t_hidden[...], t_buf[lax.rem(i, depth)], preferred_element_type=jnp.float32
            )
            if half == 0:
                sib_copy(s).start()

            @pl.when(i + depth < 2 * steps)
            def _():
                piece(i + depth).start()

        @pl.when(s == max(0, steps - 4))
        def _():
            student.start()

        @pl.when(s >= 1)
        def _():
            pair(s - 1)

        late = jnp.where(at_end, s - 1, s - lag)

        @pl.when((late >= 0) & (late < outer))
        def _():
            forward(late)

        @pl.when(s == steps // 4)
        def _():
            gather_z_wait(*hid_gather)
            start_all(gather_rest(*hid_gather))

    pair(jnp.int32(steps - 1))

    @pl.when(at_end)
    def _():
        for late in range(steps - 1, outer):
            forward(jnp.int32(late))

    left = list(range(max(0, steps - lag), outer))

    def forward_next():
        if left:
            late = left.pop(0)

            @pl.when(jnp.logical_not(at_end))
            def _():
                forward(jnp.int32(late))

    while len(left) > nq:
        forward_next()

    gather_rest_wait(*hid_gather)
    rows = s_hidden.shape[0]
    for a in range(ntt):
        for b in range(nz):
            for c in range(2):
                at = (a * nv + b * 2 + c) * rows
                hid_f[at : at + rows, :] = hid_all[c * ntt + a, b]
    hid_ref[...] = hid_f[...].astype(jnp.bfloat16)

    student.wait()

    for n in range(nq):
        logits_s[n] = jnp.dot(
            hid_ref[...], w_buf[:, n * cw : (n + 1) * cw], preferred_element_type=jnp.float32
        )
        forward_next()

    for q in range(nq):
        logits_t[q] = mine[z, q]
        for side, there in ((0, z > 0), (1, z < nz - 1)):

            @pl.when(there)
            def _():
                line_arrived(side, z, q)
                logits_t[q] += line_in[side, z, q]

    offset = (tt * nv + sv) * vd
    lanes = stat_all.shape[-1]

    square = lax.broadcasted_iota(jnp.int32, (tokens, tokens), 0) == lax.broadcasted_iota(
        jnp.int32, (tokens, tokens), 1
    )
    wanted = jnp.sum(jnp.where(square, targets[...], 0), axis=1, keepdims=True)

    def hits(q):
        columns = offset + q * cw + lax.broadcasted_iota(jnp.int32, (tokens, cw), 1)
        return (columns == wanted).astype(jnp.float32)

    def over(function, join):
        return functools.reduce(join, [function(q) for q in range(nq)])

    def add(a, b):
        return a + b

    def total(values):
        return jnp.sum(values, axis=1, keepdims=True)

    top_t = over(lambda q: jnp.max(logits_t[q], axis=1, keepdims=True), jnp.maximum)
    top_s = over(lambda q: jnp.max(logits_s[q], axis=1, keepdims=True), jnp.maximum)
    sums = [jnp.zeros((tokens, 1), jnp.float32) for _ in range(5)]
    for q in range(nq):
        lt, ls = logits_t[q] - top_t, logits_s[q]
        et = jnp.exp(lt)
        here = (et, et * ls, et * lt, jnp.exp(ls - top_s), hits(q) * ls)
        sums = [old + total(new) for old, new in zip(sums, here)]
        logits_t[q], logits_s[q] = et, here[3]
    eye = lax.broadcasted_iota(jnp.int32, (tokens, lanes), 0) == lax.broadcasted_iota(jnp.int32, (tokens, lanes), 1)

    def to_row(column):
        return jnp.sum(jnp.where(eye, column, 0.0), axis=0, keepdims=True)

    def to_column(row):
        return jnp.sum(jnp.where(eye, row, 0.0), axis=1, keepdims=True)

    stats = [top_t, sums[0], sums[1], sums[2], top_s, sums[3], sums[4]]
    stat_all[here_at, z] = jnp.concatenate(
        [to_row(x) for x in stats] + [jnp.zeros((1, lanes), jnp.float32)], axis=0
    )
    stat_gather = (stat_all, stat_send, stat_recv)
    start_all(gather_z(*stat_gather))
    hid_t_ref[...] = hid_f[...].T.astype(jnp.bfloat16)
    gather_z_wait(*stat_gather)
    start_all(gather_rest(*stat_gather))
    gather_rest_wait(*stat_gather)

    every = stat_all[...].reshape((2 * ntt * nz, 8, lanes))
    peak = jnp.max(every, axis=0)
    scale = jnp.exp(every - peak[None])
    wt, ws = scale[:, 0, :], scale[:, 4, :]
    real = lax.broadcasted_iota(jnp.int32, (1, lanes), 1) < tokens

    def joined(values):
        return jnp.where(real, jnp.sum(values, axis=0, keepdims=True), 1.0)

    sum_t = joined(wt * every[:, 1, :])
    sum_s = joined(ws * every[:, 5, :])
    log_t = jnp.log(sum_t)
    mass = joined(wt * every[:, 1, :]) / sum_t
    cross = joined(wt * every[:, 2, :]) / sum_t
    shifted = every[:, 3, :] + (every[:, 0, :] - peak[0:1]) * every[:, 1, :]
    entropy = joined(wt * shifted) / sum_t - mass * log_t
    norm_s = peak[4:5] + jnp.log(sum_s)
    picked = joined(every[:, 6, :])
    per_row = entropy - (cross - mass * norm_s) + ce_weight * (norm_s - picked)
    loss_ref[0, 0] = jnp.sum(jnp.where(real, per_row, 0.0)) / tokens

    scale_t = jnp.exp(top_t - to_column(peak[0:1] + log_t))
    scale_s = (to_column(mass) + ce_weight) * jnp.exp(top_s - to_column(norm_s))
    for q in range(nq):
        probs = (logits_t[q] * scale_t).astype(jnp.bfloat16).astype(jnp.float32)
        grad = scale_s * logits_s[q] - probs - ce_weight * hits(q)
        grad_ref[:, q * cw : (q + 1) * cw] = grad.astype(jnp.bfloat16)

    half = ds // 2
    pieces, width = hg_out.shape[0], hg_out.shape[2]
    group = tokens // ntt

    def product(who, p):
        start = pl.multiple_of(who * half + p * width, 128)
        return lax.dot_general(
            grad_ref[...], w_buf[pl.ds(start, width), :], (((1,), (1,)), ((), ())),
            preferred_element_type=jnp.float32,
        )

    def core_copy(p):
        return push(hg_out.at[p], hg_in.at[p], hg_send.at[p], hg_recv.at[p], sibling)

    def tt_copies(p):
        return [
            push(
                tt_out.at[p, other_tt(k)], tt_in.at[p, tt], tt_send.at[p, k], tt_recv.at[p, tt],
                {"tt": other_tt(k)},
            )
            for k in range(1, ntt)
        ]

    def z_copies(p):
        return [
            push(
                z_out.at[p, other_z(k)], z_in.at[p, z], z_send.at[p, k], z_recv.at[p, z],
                {"sv": other_z(k) * 2 + core},
            )
            for k in range(1, nz)
        ]

    def to_tt(p):
        core_copy(p).wait_recv()
        for a in range(ntt):
            part = slice(a * group, (a + 1) * group)
            tt_out[p, a] = hg_own[p, part, :] + hg_in[p, part, :]
        start_all(tt_copies(p))

    def to_z(p):
        here = tt_out[p, tt]
        for k in range(1, ntt):
            o = other_tt(k)
            ref = tt_in.at[p, o]
            push(ref, ref, tt_send.at[p, k], tt_recv.at[p, o], {"tt": o}).wait_recv()
            here = here + tt_in[p, o]
        for b in range(nz):
            z_out[p, b] = here[b * 2 * rows : (b + 1) * 2 * rows, :]
        start_all(z_copies(p))

    for p in range(pieces + 2):
        if p < pieces:
            hg_out[p] = product(1 - core, p)
            core_copy(p).start()
            hg_own[p] = product(core, p)
        if 1 <= p <= pieces:
            to_tt(p - 1)
        if p >= 2:
            to_z(p - 2)
    for p in range(pieces):
        here = z_out[p, z]
        for k in range(1, nz):
            o = other_z(k)
            ref = z_in.at[p, o]
            push(ref, ref, z_send.at[p, k], z_recv.at[p, o], {"sv": o * 2 + core}).wait_recv()
            here = here + z_in[p, o]
        for c in range(2):
            c_out[c, :, p * width : (p + 1) * width] = here[c * rows : (c + 1) * rows, :]
    last = push(c_out.at[1 - core], c_in, hg_send.at[pieces], hg_recv.at[pieces], sibling)
    last.start()
    hgrad_ref[:, pl.ds(pl.multiple_of(core * half, 128), half)] = c_out[core]
    last.wait_recv()
    hgrad_ref[:, pl.ds(pl.multiple_of((1 - core) * half, 128), half)] = c_in[...]

    last.wait_send()
    for p in range(pieces):
        for copy in [core_copy(p)] + tt_copies(p) + z_copies(p):
            copy.wait_send()
    gather_sent(*hid_gather)
    gather_sent(*stat_gather)

    @pl.loop(0, steps)
    def _(s):
        sib_copy(s).wait_send()

        @pl.when(s < outer)
        def _():
            line_copy(s).wait_send()


def head_kernel(hid_t_ref, grad_ref, out_ref):
    out_ref[...] = lax.dot_general(
        hid_t_ref[...], grad_ref[...], (((1,), (0,)), ((), ())), preferred_element_type=jnp.float32
    ).astype(out_ref.dtype)


def body(ntt, nv, teacher_hidden, teacher_head, student_hidden, student_head, targets):
    f32, bf16 = jnp.float32, jnp.bfloat16
    tokens, dt = teacher_hidden.shape
    rows = student_hidden.shape[0]
    ds, vd = student_head.shape
    nz = nv // 2
    cw = min(vd, 512)
    nq = vd // cw
    steps = nz * nq
    lanes = -(-tokens // 128) * 128
    half = ds // 2
    sems = pltpu.SemaphoreType.DMA
    vmem = pl.BlockSpec(memory_space=pltpu.VMEM)
    hbm = pl.BlockSpec(memory_space=pl.ANY)
    shards = (nz, nq, tokens, cw)
    peers = nz + 2 * ntt
    width = min(half, 512)
    pieces = half // width
    loss, hid_t, grad, hidden_grad = pl.pallas_call(
        functools.partial(kernel, ntt, nv, nq),
        out_shape=(
            jax.ShapeDtypeStruct((1, 1), f32),
            jax.ShapeDtypeStruct((ds, tokens), bf16),
            jax.ShapeDtypeStruct((tokens, vd), bf16),
            jax.ShapeDtypeStruct((rows, ds), f32),
        ),
        in_specs=[vmem, hbm, vmem, hbm, vmem],
        out_specs=(pl.BlockSpec(memory_space=pltpu.SMEM), vmem, vmem, vmem),
        scratch_shapes=[
            pltpu.VMEM((depth, dt, cw), bf16),
            pltpu.VMEM((ds, vd), bf16),
            pltpu.VMEM(shards, f32),
            pltpu.VMEM(shards, f32),
            pltpu.VMEM(shards, f32),
            pltpu.VMEM((2,) + shards, f32),
            pltpu.VMEM(shards[1:], f32),
            pltpu.VMEM(shards[1:], f32),
            pltpu.VMEM((2 * ntt, nz, rows, ds), f32),
            pltpu.VMEM((tokens, ds), f32),
            pltpu.VMEM((tokens, ds), bf16),
            pltpu.VMEM((2 * ntt, nz, 8, lanes), f32),
            pltpu.VMEM((pieces, tokens, width), f32),
            pltpu.VMEM((pieces, tokens, width), f32),
            pltpu.VMEM((pieces, tokens, width), f32),
            pltpu.VMEM((pieces, ntt, tokens // ntt, width), f32),
            pltpu.VMEM((pieces, ntt, tokens // ntt, width), f32),
            pltpu.VMEM((pieces, nz, 2 * rows, width), f32),
            pltpu.VMEM((pieces, nz, 2 * rows, width), f32),
            pltpu.VMEM((2, rows, half), f32),
            pltpu.VMEM((rows, half), f32),
            sems((depth,)),
            sems,
            sems((steps,)),
            sems((steps,)),
            sems((steps,)),
            sems((2, nz, nq)),
            sems((peers,)),
            sems((peers,)),
            sems((peers,)),
            sems((peers,)),
            sems((pieces + 1,)),
            sems((pieces + 1,)),
            sems((pieces, ntt)),
            sems((pieces, ntt)),
            sems((pieces, nz)),
            sems((pieces, nz)),
        ],
        compiler_params=pltpu.CompilerParams(
            collective_id=0, has_side_effects=True, vmem_limit_bytes=60 * 2**20
        ),
    )(teacher_hidden, teacher_head, student_hidden, student_head, targets.reshape(1, tokens))
    block = 512
    head_grad = pl.pallas_call(
        head_kernel,
        grid=(ds // block,),
        out_shape=jax.ShapeDtypeStruct((ds, vd), bf16),
        in_specs=[
            pl.BlockSpec((block, tokens), lambda i: (i, 0)),
            pl.BlockSpec((tokens, vd), lambda i: (0, 0)),
        ],
        out_specs=pl.BlockSpec((block, vd), lambda i: (i, 0)),
        compiler_params=pltpu.CompilerParams(vmem_limit_bytes=60 * 2**20),
    )(hid_t, grad)
    return (loss.reshape(()), head_grad, hidden_grad)


def solution(mesh):
    placed = (P(None, "sv"), P("sv", "tt"), P(("tt", "sv"), None), P(None, ("tt", "sv")), P())
    return jax.shard_map(
        functools.partial(body, mesh.shape["tt"], mesh.shape["sv"]),
        mesh=mesh,
        in_specs=placed,
        out_specs=(P(), P(None, ("tt", "sv")), P(("tt", "sv"), None)),
        check_vma=False,
    )
```

time: 88.5 us -> 86.1 us (0.973)
  local copies, waits for them, and re-layouts: 3.96 us -> 0.62 us
    unnamed x7 -> x3, local copies, waits for them, and re-layouts: 2.61 us -> 0.62 us
    reshape x1 -> x0, local copies, waits for them, and re-layouts: 1.36 us -> none  [body(): targets.reshape(tokens, 1)]
    pallas_call x1, Pallas kernels: 8.98 us -> 10.1 us  [body(): pl.pallas_call(head_kernel, grid=(ds // block,), out_shape=jax.ShapeDtype...]
where the time goes in v2:
time: 86.1 us; the launch traced here: 85.8 us
  Pallas kernels  82.8 us (96%)
  between operations  2.42 us (3%)
    pallas_call x1, Pallas kernels, body(): pl.pallas_call(functools.partial(kernel, ntt, nv, nq), out_shape=(jax.Sha...  72.7 us
    pallas_call x1, Pallas kernels, body(): pl.pallas_call(head_kernel, grid=(ds // block,), out_shape=jax.ShapeDtype...  10.1 us

profile of v2, /device:TPU:0, one launch (start us, length us, event | category | flops | bytes accessed | tf_op | source)
XLA Modules:
  0.0 85.8 jit_solution(16695281752026043209)
XLA Ops:
  0.6 72.7 %shard_map.76 = (f32[1,1]{1,0:T(1,128)}, bf16[4096,64]{1,0:T(8,128)(2,1)}, bf16[64,2048]{1,0:T(8,128)(2,1)}, f32[2,4096]{1,0:T(2,128)}) custom-call(bf16[64,2048]{1,0:T(8,128)(2,1)} %t_hidden.1, bf16[2048,16384]{1,0:T(8,128)(2,1)} %t_head.1, bf16[2,4096]{1,0:T(2,128)(2,1)} %s_hidden.1, bf16[4096,2048]{1,0:T(8,128)(2,1)} %s_head.1, s32[1,64]{1,0:T(1,128)} %bitcast.2), custom_call_target="tpu_custom_call" | custom-call | tf_op jit(solution)/shard_map/pallas_call | solution.py:443
  73.3 0.0 copy-start
  73.3 10.1 %shard_map.77 = bf16[4096,2048]{1,0:T(8,128)(2,1)} custom-call(bf16[4096,64]{1,0:T(8,128)(2,1)} %get-tuple-element.8.hid_t_ref, bf16[64,2048]{1,0:T(8,128)(2,1)} %get-tuple-element.9.grad_ref), custom_call_target="tpu_custom_call" | custom-call | tf_op jit(solution)/shard_map/pallas_call | solution.py:497
  84.0 0.0 copy-done
  84.1 0.6 copy.11
Async XLA Ops:
  73.3 10.7 %copy-start = (f32[2,4096]{1,0:T(2,128)S(1)}, f32[2,4096]{1,0:T(2,128)}, u32[]{:S(2)}) copy-start(f32[2,4096]{1,0:T(2,128)} %get-tuple-element.16) | copy-start | bytes 98308

commit v3 on v2

--- a/solution.py
+++ b/solution.py
@@ -42,7 +42,7 @@
     t_hidden, t_head, s_hidden, s_head, targets,
     loss_ref, hid_t_ref, grad_ref, hgrad_ref,
     t_buf, w_buf, mine, sib_out, sib_in, line_in, logits_t, logits_s,
-    hid_all, hid_f, hid_ref, stat_all, hg_out, hg_in, hg_own, tt_out, tt_in, z_out, z_in, c_out, c_in,
+    hid_all, hid_f, hid_ref, grad_t, stat_all, hg_out, hg_in, hg_own, tt_out, tt_in, z_out, z_in, c_out, c_in,
     t_sem, w_sem, sib_send, sib_recv, line_send, line_recv,
     hid_send, hid_recv, stat_send, stat_recv, hg_send, hg_recv, tt_send, tt_recv, z_send, z_recv,
 ):
@@ -325,6 +325,7 @@
         probs = (logits_t[q] * scale_t).astype(jnp.bfloat16).astype(jnp.float32)
         grad = scale_s * logits_s[q] - probs - ce_weight * hits(q)
         grad_ref[:, q * cw : (q + 1) * cw] = grad.astype(jnp.bfloat16)
+        grad_t[q * cw : (q + 1) * cw, :] = grad.T.astype(jnp.bfloat16)
 
     half = ds // 2
     pieces, width = hg_out.shape[0], hg_out.shape[2]
@@ -332,10 +333,7 @@
 
     def product(who, p):
         start = pl.multiple_of(who * half + p * width, 128)
-        return lax.dot_general(
-            grad_ref[...], w_buf[pl.ds(start, width), :], (((1,), (1,)), ((), ())),
-            preferred_element_type=jnp.float32,
-        )
+        return jnp.dot(w_buf[pl.ds(start, width), :], grad_t[...], preferred_element_type=jnp.float32).T
 
     def core_copy(p):
         return push(hg_out.at[p], hg_in.at[p], hg_send.at[p], hg_recv.at[p], sibling)
@@ -417,9 +415,12 @@
 
 
 def head_kernel(hid_t_ref, grad_ref, out_ref):
-    out_ref[...] = lax.dot_general(
-        hid_t_ref[...], grad_ref[...], (((1,), (0,)), ((), ())), preferred_element_type=jnp.float32
-    ).astype(out_ref.dtype)
+    tile = 256
+    for n in range(out_ref.shape[1] // tile):
+        part = slice(n * tile, (n + 1) * tile)
+        out_ref[:, part] = jnp.dot(
+            hid_t_ref[...], grad_ref[:, part], preferred_element_type=jnp.float32
+        ).astype(out_ref.dtype)
 
 
 def body(ntt, nv, teacher_hidden, teacher_head, student_hidden, student_head, targets):
@@ -462,6 +463,7 @@
             pltpu.VMEM((2 * ntt, nz, rows, ds), f32),
             pltpu.VMEM((tokens, ds), f32),
             pltpu.VMEM((tokens, ds), bf16),
+            pltpu.VMEM((vd, tokens), bf16),
             pltpu.VMEM((2 * ntt, nz, 8, lanes), f32),
             pltpu.VMEM((pieces, tokens, width), f32),
             pltpu.VMEM((pieces, tokens, width), f32),
@@ -493,7 +495,7 @@
             collective_id=0, has_side_effects=True, vmem_limit_bytes=60 * 2**20
         ),
     )(teacher_hidden, teacher_head, student_hidden, student_head, targets.reshape(1, tokens))
-    block = 512
+    block = 256
     head_grad = pl.pallas_call(
         head_kernel,
         grid=(ds // block,),

time: 86.1 us -> 91.4 us (1.062)
  Pallas kernels: 82.8 us -> 87.5 us
    pallas_call x1, Pallas kernels: 10.1 us -> 13.6 us  [body(): pl.pallas_call(head_kernel, grid=(ds // block,), out_shape=jax.ShapeDtype...]
    pallas_call x1, Pallas kernels: 72.7 us -> 73.9 us  [body(): pl.pallas_call(functools.partial(kernel, ntt, nv, nq), out_shape=(jax.Sha...]
where the time goes in v3:
time: 91.4 us; the launch traced here: 90.5 us
  Pallas kernels  87.5 us (96%)
  between operations  2.42 us (3%)
    pallas_call x1, Pallas kernels, body(): pl.pallas_call(functools.partial(kernel, ntt, nv, nq), out_shape=(jax.Sha...  73.9 us
    pallas_call x1, Pallas kernels, body(): pl.pallas_call(head_kernel, grid=(ds // block,), out_shape=jax.ShapeDtype...  13.6 us

profile of v3, /device:TPU:0, one launch (start us, length us, event | category | flops | bytes accessed | tf_op | source)
XLA Modules:
  0.0 90.5 jit_solution(4116667606375606700)
XLA Ops:
  0.6 73.9 %shard_map.76 = (f32[1,1]{1,0:T(1,128)}, bf16[4096,64]{1,0:T(8,128)(2,1)}, bf16[64,2048]{1,0:T(8,128)(2,1)}, f32[2,4096]{1,0:T(2,128)}) custom-call(bf16[64,2048]{1,0:T(8,128)(2,1)} %t_hidden.1, bf16[2048,16384]{1,0:T(8,128)(2,1)} %t_head.1, bf16[2,4096]{1,0:T(2,128)(2,1)} %s_hidden.1, bf16[4096,2048]{1,0:T(8,128)(2,1)} %s_head.1, s32[1,64]{1,0:T(1,128)} %bitcast.2), custom_call_target="tpu_custom_call" | custom-call | tf_op jit(solution)/shard_map/pallas_call | solution.py:444
  74.5 0.0 copy-start
  74.5 13.6 %shard_map.77 = bf16[4096,2048]{1,0:T(8,128)(2,1)} custom-call(bf16[4096,64]{1,0:T(8,128)(2,1)} %get-tuple-element.8.hid_t_ref, bf16[64,2048]{1,0:T(8,128)(2,1)} %get-tuple-element.9.grad_ref), custom_call_target="tpu_custom_call" | custom-call | tf_op jit(solution)/shard_map/pallas_call | solution.py:499
  88.8 0.0 copy-done
  88.8 0.6 copy.11
Async XLA Ops:
  74.5 14.3 %copy-start = (f32[2,4096]{1,0:T(2,128)S(1)}, f32[2,4096]{1,0:T(2,128)}, u32[]{:S(2)}) copy-start(f32[2,4096]{1,0:T(2,128)} %get-tuple-element.16) | copy-start | bytes 98308
